TPU v7x, 32 devices: a whole 2x2x4 slice. The times are simulated.
32 devices in a mesh: groups: 2 (over y), seq: 4 (over z), head: 2 (over x), hsub: 2 (over core).
Axes of the slice: x: 2, y: 2, z: 4, core: 2. Of those that a mesh axis runs over, the one named last changes fastest.
Arguments:
- token_values: bfloat16 [16384, 2048], P(('groups', 'seq'), ('head', 'hsub')), parts along dimension 0, may hold values from -0.125 to 0.125
- key_proj: bfloat16 [16384, 128], P(('groups', 'seq')), parts along dimension 0, may hold values from -0.5 to 0.5
- query_proj: bfloat16 [16384, 128], P(('groups', 'seq')), parts along dimension 0, may hold values from -0.5 to 0.5
- log_decay: float32 [32, 16384], P(('head', 'hsub'), ('groups', 'seq')), parts along dimension 1, may hold values from 0 to 2, as said below
- out_grad: bfloat16 [16384, 2048], P(('groups', 'seq'), ('head', 'hsub')), parts along dimension 0, may hold values from -6 to 6
Outputs:
- value_grad: bfloat16 [16384, 2048], P(('groups', 'seq'), ('head', 'hsub')), parts along dimension 0
- key_grad: float32 [16384, 128], P(('groups', 'seq', 'head', 'hsub')), parts along dimension 0
- query_grad: float32 [16384, 128], P(('groups', 'seq', 'head', 'hsub')), parts along dimension 0
There are 2 independent parts, one for each index of `groups`. A program takes and returns all parts, laid end to end along the dimension named above; each array names one. Nothing has to cross between parts.
Inputs may be any that keep to these rules, and one draw needn't show every extreme that they name: log_decay is positive.
All inputs are finite; a program needn't handle non-finite values.
Results may differ from a plain program's by a relative error of at most 0.0057.
Values sent between devices are 32-bit elements; how exact they have to be, the bound alone decides.
A program may use at most 128 MiB of HBM per device.

v0:
```python
import jax
import jax.numpy as jnp
from jax import lax
from jax.sharding import PartitionSpec as P

BLOCK = 128


def carried_in(x, axis, combine, identity, reverse):
    devices, mine = (lax.axis_size(axis), lax.axis_index(axis))
    everything = jax.tree.map(lambda part: lax.all_gather(part, axis), x)
    start = jax.tree.map(
        lambda part, zero: jnp.broadcast_to(jnp.asarray(zero, part.dtype), part.shape), x, identity
    )

    def hop(k, before):
        at = devices - 1 - k if reverse else k
        reached = at > mine if reverse else at < mine
        new = combine(before, jax.tree.map(lambda part: part[at], everything))
        return jax.tree.map(lambda a, b: jnp.where(reached, a, b), new, before)

    return lax.fori_loop(0, devices, hop, start)


def link_states(earlier, later):
    return (earlier[0] * later[0], later[0][:, None, None] * earlier[1] + later[1])


def advance(carry, pieces):
    return (pieces[0][:, None, None] * carry + pieces[1], carry)


def local(token_values, key_proj, query_proj, log_decay, out_grad):
    wide = jnp.float32
    length = token_values.shape[0]
    heads = log_decay.shape[0]
    channels = token_values.shape[1] // heads
    state_size = key_proj.shape[1]
    count = length // BLOCK
    key_rows = key_proj.reshape(count, BLOCK, state_size)
    query_rows = query_proj.reshape(count, BLOCK, state_size)
    values = token_values.reshape(count, BLOCK, heads, channels)
    grads = out_grad.reshape(count, BLOCK, heads, channels)
    scores = jnp.einsum("cin,cjn->cij", query_rows, key_rows, preferred_element_type=wide)
    within = jnp.cumsum(log_decay.reshape(heads, count, BLOCK), axis=2)
    block_last = within[:, :, -1]
    positions = jnp.arange(BLOCK)
    causal = positions[:, None] >= positions[None, :]
    inside = within[:, :, :, None] - within[:, :, None, :]
    decay_mask = jnp.exp(-jnp.where(causal[None, None], inside, jnp.inf))
    mixed = (decay_mask * scores[None]).astype(jnp.bfloat16)
    pairs = jnp.einsum("cihp,cjhp->hcij", grads, values, preferred_element_type=wide)
    pair_mask = (decay_mask * pairs).astype(jnp.bfloat16)
    tail_weight = jnp.exp(within - block_last[:, :, None])
    lead_weight = jnp.exp(-within)
    tail_keys = (tail_weight[..., None] * key_rows.astype(wide)[None]).astype(jnp.bfloat16)
    lead_queries = (lead_weight[..., None] * query_rows.astype(wide)[None]).astype(jnp.bfloat16)
    block_states = jnp.einsum("hcjn,cjhp->chnp", tail_keys, values, preferred_element_type=wide)
    block_adjoints = jnp.einsum("hcin,cihp->chnp", lead_queries, grads, preferred_element_type=wide)
    decays = jnp.transpose(jnp.exp(-block_last))
    zero_state = jnp.zeros((heads, state_size, channels), wide)
    own_state, local_entering = lax.scan(advance, zero_state, (decays, block_states))
    own_adjoint, local_after = lax.scan(advance, zero_state, (decays, block_adjoints), reverse=True)
    through = jnp.cumsum(block_last, axis=1)
    total = through[:, -1]
    decay_total = jnp.exp(-total)
    identity = (jnp.ones_like(decay_total), jnp.zeros_like(own_state))
    start_state = carried_in((decay_total, own_state), "seq", link_states, identity, False)[1]
    incoming = carried_in((decay_total, own_adjoint), "seq", link_states, identity, True)[1]
    before_weight = jnp.transpose(jnp.exp(-(through - block_last)))
    onward_weight = jnp.transpose(jnp.exp(-(total[:, None] - through)))
    entering = local_entering + before_weight[:, :, None, None] * start_state[None]
    after = local_after + onward_weight[:, :, None, None] * incoming[None]
    entering_low = entering.astype(jnp.bfloat16)
    after_low = after.astype(jnp.bfloat16)
    tail_order = jnp.transpose(tail_weight, (1, 2, 0))[..., None]
    lead_order = jnp.transpose(lead_weight, (1, 2, 0))[..., None]
    value_part = jnp.einsum("hcij,cihp->cjhp", mixed, grads, preferred_element_type=wide)
    value_part = value_part + tail_order * jnp.einsum(
        "cjn,chnp->cjhp", key_rows, after_low, preferred_element_type=wide
    )
    key_part = jnp.einsum("hcij,cin->cjn", pair_mask, query_rows, preferred_element_type=wide)
    key_carried = jnp.einsum("cjhp,chnp->cjhn", values, after_low, preferred_element_type=wide)
    key_part = key_part + jnp.sum(tail_order * key_carried, axis=2)
    query_part = jnp.einsum("hcij,cjn->cin", pair_mask, key_rows, preferred_element_type=wide)
    query_carried = jnp.einsum("cihp,chnp->cihn", grads, entering_low, preferred_element_type=wide)
    query_part = query_part + jnp.sum(lead_order * query_carried, axis=2)
    value_grad = value_part.reshape(length, heads * channels).astype(jnp.bfloat16)
    key_grad, query_grad = (
        lax.psum_scatter(
            key_part.reshape(length, state_size), ("head", "hsub"), scatter_dimension=0, tiled=True
        ),
        lax.psum_scatter(
            query_part.reshape(length, state_size),
            ("head", "hsub"),
            scatter_dimension=0,
            tiled=True,
        ),
    )
    return (value_grad, key_grad, query_grad)


def solution(mesh):
    placed = (
        P(("groups", "seq"), ("head", "hsub")),
        P(("groups", "seq"), None),
        P(("groups", "seq"), None),
        P(("head", "hsub"), ("groups", "seq")),
        P(("groups", "seq"), ("head", "hsub")),
    )
    return jax.shard_map(
        local,
        mesh=mesh,
        in_specs=placed,
        out_specs=(
            P(("groups", "seq"), ("head", "hsub")),
            P(("groups", "seq", "head", "hsub"), None),
            P(("groups", "seq", "head", "hsub"), None),
        ),
        check_vma=False,
    )
```

profile of v0, /device:TPU:0, one launch (start us, length us, event | category | flops | bytes accessed | tf_op | source)
XLA Modules:
  0.0 206.6 jit_solution(5991788634647135218)
XLA Ops:
  8.1 2.3 %reduce_window_sum.24 = f32[8,16,128]{2,1,0:T(8,128)S(1)} reduce-window(f32[8,16,128]{2,1,0:T(8,128)S(1)} %copy.60, f32[]{:T(128)} %constant.125.clone.1), window={size=1x1x128 pad=0_0x0_0x127_0}, to_apply=%region_0.0 | reduce-window | flops 2080768 | bytes 131076 | tf_op jit(solution)/shard_map/jit(cumsum)/reduce_window_sum | solution.py:45
  11.2 2.9 %copy.74 = bf16[2048,512]{0,1:T(8,128)(2,1)S(1)} copy(bf16[2048,512]{1,0:T(8,128)(2,1)} %param.13) | data formatting | bytes 4194304 | tf_op args[0]
  14.2 2.0 copy.106
  16.3 8.0 %fusion.7 = f32[16,8,128,64]{3,2,1,0:T(8,128)} fusion(f32[16,128,128]{2,1,0:T(8,128)S(1)} %convert_element_type.50, f32[8,16,128]{2,0,1:T(8,128)S(1)} %copy.83, bf16[16,128,8,64]{1,0,3,2:T(8,128)(2,1)} %bitcast.113), kind=kOutput, calls=%fused_computation.29 | convolution fusion | flops 272629760 | bytes 7405568 | tf_op jit(solution)/shard_map/hcjn,cjhp->chnp/dot_general | solution.py:58
  24.3 4.3 %broadcast.28.clone.1 = f32[16,8,128,64]{3,2,1,0:T(8,128)} broadcast(f32[]{:T(128)} %constant.125.clone.1), dimensions={} | broadcast | bytes 4194308 | tf_op jit(solution)/shard_map/broadcast.2
  28.6 32.5 %while.62 = (s32[]{:T(128)}, f32[8,128,64]{2,1,0:T(8,128)S(1)}, f32[16,8,128,64]{3,2,1,0:T(8,128)}, f32[16,8]{1,0:T(8,128)S(1)}, f32[16,8,128,64]{3,2,1,0:T(8,128)}, /*index=5*/s32[]{:T(128)}, s32[]{:T(128)}) while((s32[]{:T(128)}, f32[8,128,64]{2,1,0:T(8,128)S(1)}, f32[16,8,128,64]{3,2,1,0:T(8,128)}, f32[16,8]{1,0:T(8,128)S(1)}, ...), condition=%wide.region_10.11_spmd.clone, body=%wide.region_9.10_spmd.clone.sunk | while | flops 262147 | bytes 1573568 | solution.py:62
  29.4 1.2 bitcast_add_fusion.7
  31.5 1.2 bitcast_add_fusion.7
  33.5 1.2 bitcast_add_fusion.7
  35.5 1.2 bitcast_add_fusion.7
  37.6 1.2 bitcast_add_fusion.7
  39.6 1.2 bitcast_add_fusion.7
  41.6 1.2 bitcast_add_fusion.7
  43.6 1.2 bitcast_add_fusion.7
  45.7 1.2 bitcast_add_fusion.7
  47.7 1.2 bitcast_add_fusion.7
  49.7 1.2 bitcast_add_fusion.7
  51.8 1.2 bitcast_add_fusion.7
  53.8 1.2 bitcast_add_fusion.7
  55.9 1.2 bitcast_add_fusion.7
  57.9 1.2 bitcast_add_fusion.7
  59.9 1.2 bitcast_add_fusion.7
  62.1 2.9 %copy.61 = bf16[2048,512]{0,1:T(8,128)(2,1)S(1)} copy(bf16[2048,512]{1,0:T(8,128)(2,1)} %param.17) | data formatting | bytes 4194304 | tf_op args[4]
  65.7 1.5 convert_element_type.43
  67.2 6.6 %fusion.6 = f32[16,8,128,64]{3,2,1,0:T(8,128)} fusion(f32[16,128,128]{2,1,0:T(8,128)S(1)} %convert_element_type.43, f32[8,16,128]{2,0,1:T(8,128)S(1)} %copy.65, bf16[16,128,8,64]{1,0,3,2:T(8,128)(2,1)S(1)} %bitcast.116), kind=kOutput, calls=%fused_computation.28 | convolution fusion | flops 272629760 | bytes 7405568 | tf_op jit(solution)/shard_map/hcin,cihp->chnp/dot_general | solution.py:59
  73.8 4.3 %broadcast.28.clone = f32[16,8,128,64]{3,2,1,0:T(8,128)} broadcast(f32[]{:T(128)} %constant.125.clone.1), dimensions={} | broadcast | bytes 4194308 | tf_op jit(solution)/shard_map/broadcast.2
  78.1 32.6 %while.60 = (s32[]{:T(128)}, f32[8,128,64]{2,1,0:T(8,128)S(1)}, f32[16,8,128,64]{3,2,1,0:T(8,128)}, f32[16,8]{1,0:T(8,128)S(1)}, f32[16,8,128,64]{3,2,1,0:T(8,128)}, /*index=5*/s32[]{:T(128)}, s32[]{:T(128)}, s32[]{:T(128)}) while((s32[]{:T(128)}, f32[8,128,64]{2,1,0:T(8,128)S(1)}, f32[16,8,128,64]{3,2,1,0:T(8,128)}, ...), condition=%wide.region_2.3_spmd.clone, body=%wide.region_1.2_spmd.clone.sunk | while | flops 262148 | bytes 1573080 | solution.py:63
  78.9 1.2 bitcast_add_fusion.6
  81.0 1.2 bitcast_add_fusion.6
  83.0 1.2 bitcast_add_fusion.6
  85.0 1.2 bitcast_add_fusion.6
  87.1 1.2 bitcast_add_fusion.6
  89.1 1.2 bitcast_add_fusion.6
  91.2 1.2 bitcast_add_fusion.6
  93.2 1.2 bitcast_add_fusion.6
  95.2 1.2 bitcast_add_fusion.6
  97.3 1.2 bitcast_add_fusion.6
  99.3 1.2 bitcast_add_fusion.6
  101.4 1.2 bitcast_add_fusion.6
  103.4 1.2 bitcast_add_fusion.6
  105.4 1.2 bitcast_add_fusion.6
  107.5 1.2 bitcast_add_fusion.6
  109.6 1.2 bitcast_add_fusion.6
  113.4 13.7 %all-reduce = f32[32]{0:T(128)S(1)} all-reduce(f32[32]{0:T(128)S(1)} %dynamic-update-slice), channel_id=2, replica_groups=mesh['groups'=2,'seq'=4,'head'=2,'hsub'=2] {'seq'}, use_global_device_ids=true, to_apply=%add | all-reduce | flops 32 | bytes 256
  127.3 5.6 %convert_reduce_fusion = bf16[16,128,128]{2,1,0:T(8,128)(2,1)S(1)} fusion(f32[8,16,128]{2,1,0:T(8,128)S(1)} %reduce_window_sum.24, pred[128,128]{1,0:T(8,128)(4,1)S(1)} %iota_compare_fusion, bf16[16,128,8,64]{1,0,3,2:T(8,128)(2,1)} %bitcast.114, bf16[16,128,8,64]{1,0,3,2:T(8,128)(2,1)} %bitcast.117), kind=kOutput, calls=%fused_computation.22 | convolution fusion | flops 282853376 | bytes 4800512 | tf_op jit(solution)/shard_map/cihp,cjhp->hcij/dot_general | solution.py:52
  133.1 5.5 %while.63 = (s32[]{:T(128)}, f32[8,128,64]{2,1,0:T(8,128)S(1)}, s32[]{:T(128)}, f32[4,8]{1,0:T(4,128)S(1)}, f32[4,8,128,64]{2,3,1,0:T(8,128)}, /*index=5*/s32[]{:T(128)}, s32[]{:T(128)}) while((s32[]{:T(128)}, f32[8,128,64]{2,1,0:T(8,128)S(1)}, s32[]{:T(128)}, f32[4,8]{1,0:T(4,128)S(1)}, f32[4,8,128,64]{2,3,1,0:T(8,128)}, ...), condition=%wide.region_12.13_spmd.clone, body=%wide.region_11.12_spmd.clone.sunk | while | flops 262148 | bytes 1835209 | solution.py:22
  133.1 1.0 constant_dynamic-slice_fusion.7
  138.6 7.4 %fusion.4 = f32[16,128,128]{1,2,0:T(8,128)} fusion(f32[16,128,8]{1,2,0:T(8,128)S(1)} %copy.82, f32[16,8,128,64]{3,2,1,0:T(8,128)} %get-tuple-element.364, f32[8,128,64]{2,1,0:T(8,128)S(1)} %get-tuple-element.366, f32[16,8]{1,0:T(8,128)S(1)} %copy.87, bf16[16,128,8,64]{1,0,3,2:T(8,128)(2,1)} %bitcast.118), kind=kOutput, calls=%fused_computation.17 | convolution fusion | flops 275513344 | bytes 7668224 | tf_op jit(solution)/shard_map/cihp,chnp->cihn/dot_general | solution.py:86
  145.9 1.6 copy.92
  147.5 1.3 convolution_add_fusion
  149.1 5.5 %while.61 = (s32[]{:T(128)}, f32[8,128,64]{2,1,0:T(8,128)S(1)}, s32[]{:T(128)}, f32[4,8]{1,0:T(4,128)S(1)}, f32[4,8,128,64]{2,3,1,0:T(8,128)}, /*index=5*/s32[]{:T(128)}, s32[]{:T(128)}, s32[]{:T(128)}, s32[]{:T(128)}) while((s32[]{:T(128)}, f32[8,128,64]{2,1,0:T(8,128)S(1)}, s32[]{:T(128)}, f32[4,8]{1,0:T(4,128)S(1)}, ...), condition=%wide.region_5.6_spmd.clone, body=%wide.region_4.5_spmd.clone.sunk | while | flops 262152 | bytes 1835271 | solution.py:22
  149.1 1.0 constant_dynamic-slice_fusion.6
  150.5 1.0 constant_dynamic-slice_fusion.6
  151.9 1.0 constant_dynamic-slice_fusion.6
  153.2 1.0 constant_dynamic-slice_fusion.6
  154.6 7.6 %fusion.5 = f32[16,128,128]{1,2,0:T(8,128)} fusion(f32[16,128,8]{1,2,0:T(8,128)S(1)} %copy.64, bf16[16,128,8,64]{1,0,3,2:T(8,128)(2,1)} %bitcast.115, f32[16,8,128,64]{3,2,1,0:T(8,128)} %get-tuple-element.361, f32[8,128,64]{2,1,0:T(8,128)S(1)} %get-tuple-element.363, f32[16,8]{1,0:T(8,128)S(1)} %copy.69), kind=kOutput, calls=%fused_computation.19 | convolution fusion | flops 275513344 | bytes 7668224 | tf_op jit(solution)/shard_map/cjhp,chnp->cjhn/dot_general | solution.py:83
  162.2 2.6 %copy.81 = f32[16,128,128]{2,1,0:T(8,128)} copy(f32[16,128,128]{1,2,0:T(8,128)} %fusion.5) | data formatting | bytes 2097152 | tf_op jit(solution)/shard_map/reduce_sum | solution.py:84
  164.7 2.9 %convolution_add_fusion.1 = f32[16,128,128]{2,1,0:T(8,128)} fusion(f32[16,128,128]{2,1,0:T(8,128)} %copy.81, bf16[16,128,128]{2,1,0:T(8,128)(2,1)} %copy-done.3, bf16[16,128,128]{2,1,0:T(8,128)(2,1)} %bitcast.121), kind=kOutput, calls=%fused_computation.50 | convolution fusion | flops 67371008 | bytes 3145728 | tf_op jit(solution)/shard_map/hcij,cin->cjn/dot_general | solution.py:82
  167.7 1.7 fusion.28
  169.4 2.5 %fusion.11 = f32[16,8,128,64]{2,3,1,0:T(8,128)S(1)} fusion(bf16[16,128,8,64]{1,0,3,2:T(8,128)(2,1)S(1)} %bitcast.119, f32[16,128,128]{2,1,0:T(8,128)S(1)} %fusion.28, f32[8,16,128]{2,1,0:T(8,128)S(1)} %reduce_window_sum.24, pred[128,128]{1,0:T(8,128)(4,1)S(1)} %iota_compare_fusion), kind=kOutput, calls=%fused_computation.34 | convolution fusion | flops 278921216 | bytes 7421952 | tf_op jit(solution)/shard_map/hcij,cihp->cjhp/dot_general | solution.py:78
  171.9 2.7 %fusion.10 = bf16[16,128,8,64]{1,3,2,0:T(8,128)(2,1)S(1)} fusion(f32[16,8,128,64]{2,3,1,0:T(8,128)S(1)} %fusion.11, bf16[16,128,128,1]{2,1,3,0:T(8,128)(2,1)S(1)} %bitcast.112, f32[16,128,8]{1,2,0:T(8,128)S(1)} %copy.64, f32[16,8,128,64]{3,2,1,0:T(8,128)S(1)} %bitcast.106, f32[8,128,64]{2,1,0:T(8,128)S(1)} %get-tuple-element.363, f32[16,8]{1,0:T(8,128)S(1)} %copy.69), kind=kOutput, calls=%fused_computation.33 | convolution fusion | flops 274726912 | bytes 11338240 | tf_op jit(solution)/shard_map/cjn,chnp->cjhp/dot_general | solution.py:79
  174.5 3.6 %copy.101 = bf16[16,128,8,64]{3,2,1,0:T(8,128)(2,1)} copy(bf16[16,128,8,64]{1,3,2,0:T(8,128)(2,1)S(1)} %fusion.10) | data formatting | bytes 4194304
  178.1 6.5 %reshape.106 = bf16[2048,512]{1,0:T(8,128)(2,1)} reshape(bf16[16,128,8,64]{3,2,1,0:T(8,128)(2,1)} %copy.101) | data formatting | bytes 4194304
  184.6 15.5 %reduce-scatter.3.cloned.1.call-done = f32[512,128]{1,0:T(8,128)} async-done(((f32[2048,128]{1,0:T(8,128)}), f32[512,128]{1,0:T(8,128)}) %reduce-scatter.3.cloned.1.call-update) | async-done | bytes 262160 | tf_op jit(solution)/shard_map/reduce_scatter | solution.py:90
  (144 shorter events, 39.1 us)
Async XLA Ops:
  7.2 9.0 %copy-start = (bf16[2048,128]{1,0:T(8,128)(2,1)S(1)}, bf16[2048,128]{1,0:T(8,128)(2,1)}, u32[]{:S(2)}) copy-start(bf16[2048,128]{1,0:T(8,128)(2,1)} %param.14) | copy-start | bytes 1572868
  7.2 125.9 %all-gather.8.cloned.1.call-start = ((), (), s32[]{:S(2)}) async-start(), calls=%async_computation.5 | async-start | bytes 1310720 | tf_op jit(solution)/shard_map/all_gather | solution.py:11
  62.0 87.1 %all-gather.6.cloned.1.call-start = ((), (), s32[]{:S(2)}) async-start(), calls=%async_computation.4 | async-start | bytes 1310720 | tf_op jit(solution)/shard_map/all_gather | solution.py:11
  65.6 12.5 %copy-start.1 = (bf16[64,8,16,128]{3,2,1,0:T(8,128)(2,1)}, bf16[64,8,16,128]{3,2,1,0:T(8,128)(2,1)S(1)}, u32[]{:S(2)}) copy-start(bf16[64,8,16,128]{3,2,1,0:T(8,128)(2,1)S(1)} %copy.105) | copy-start | bytes 6291460
  78.1 33.7 %copy-start.4 = (u32[32]{0:T(128)S(1)}, u32[32]{0:T(128)}, u32[]{:S(2)}) copy-start(u32[32]{0:T(128)} %constant.132) | copy-start | bytes 388
  111.7 73.0 %reduce-scatter.5.cloned.1.call-start = ((), (), s32[]{:S(2)}) async-start(), calls=%async_computation.3 | async-start | bytes 1310720 | tf_op jit(solution)/shard_map/reduce_scatter | solution.py:93
  133.0 14.5 %copy-start.3 = (bf16[16,128,128]{2,1,0:T(8,128)(2,1)}, bf16[16,128,128]{2,1,0:T(8,128)(2,1)S(1)}, u32[]{:S(2)}) copy-start(bf16[16,128,128]{2,1,0:T(8,128)(2,1)S(1)} %convert_reduce_fusion) | copy-start | bytes 1572868
  148.8 51.3 %reduce-scatter.3.cloned.1.call-start = ((), (), s32[]{:S(2)}) async-start(), calls=%async_computation.2 | async-start | bytes 1310720 | tf_op jit(solution)/shard_map/reduce_scatter | solution.py:90
  154.6 14.8 %copy-start.2 = (bf16[64,8,16,128]{3,2,1,0:T(8,128)(2,1)S(1)}, bf16[64,8,16,128]{3,2,1,0:T(8,128)(2,1)}, u32[]{:S(2)}) copy-start(bf16[64,8,16,128]{3,2,1,0:T(8,128)(2,1)} %copy-done.1) | copy-start | bytes 6291460
  167.7 4.2 %slice-start = ((s8[8388608]{0:T(1024)(128)(4,1)}), s8[4194304]{0:T(1024)(128)(4,1)S(1)}, s32[]{:S(2)}) async-start(s8[8388608]{0:T(1024)(128)(4,1)} %bitcast.105), calls=%async_computation.6 | async-start | bytes 8388608
  169.4 2.5 %slice-start.1 = ((s8[8388608]{0:T(1024)(128)(4,1)}), s8[4194304]{0:T(1024)(128)(4,1)S(1)}, s32[]{:S(2)}) async-start(s8[8388608]{0:T(1024)(128)(4,1)} %bitcast.105), calls=%async_computation.7 | async-start | bytes 8388608
Sparse Core Ops, SparseCore 0:
  62.1 30.6 all-gather.7
  111.8 30.6 all-gather.5
  148.9 23.0 reduce-scatter.4
  175.2 24.8 reduce-scatter.2
where the time goes:
time: 209 us; the launch traced here: 207 us
  other arithmetic  69.8 us (33%)
  matrix products  46.1 us (22%)
  local copies, waits for them, and re-layouts  45.1 us (22%)
  waiting for transfers between devices  15.6 us (7%)
  between operations  14.8 us (7%)
  blocking collectives  13.7 us (7%)
    add x32, other arithmetic, advance(): return (pieces[0][:, None, None] * carry + pieces[1], carry)  37.1 us
    dynamic_update_slice x32, other arithmetic, local(): lax.scan(advance, zero_state, (decays, block_states))  27.2 us
    unnamed x24, local copies, waits for them, and re-layouts  19.6 us
    reduce_scatter x1, waiting for transfers between devices, local(): lax.psum_scatter(key_part.reshape(length, state_size), ('head', 'hsub'),...  15.5 us
    unnamed x1, blocking collectives  13.7 us
    dynamic_slice x16, local copies, waits for them, and re-layouts, hop(): new = combine(before, jax.tree.map(lambda part: part[at], everything))  9.44 us
    another operation x2, local copies, waits for them, and re-layouts  8.54 us
    dot_general x1, matrix products, local(): jnp.einsum('hcjn,cjhp->chnp', tail_keys, values, preferred_element_type=w...  8 us
  transfers between devices with their start and end apart: 4, of which 1 were waited for; matrix products, arithmetic and copies ran while one was open for 52% of the time, Pallas kernels for 0%

commit v1 on v0

v1 whole, which is shorter than its diff:
```python
import functools
import jax
import jax.numpy as jnp
from jax import lax
from jax.experimental import pallas as pl
from jax.experimental.pallas import tpu as pltpu
from jax.sharding import PartitionSpec as P

BLOCK = 128
LANES = 128
WIDE = jnp.float32
LOW = jnp.bfloat16
MESH = pl.DeviceIdType.MESH


def product(a, b, over):
    return lax.dot_general(a, b, (((over[0],), (over[1],)), ((), ())), preferred_element_type=WIDE)


def kernel(
    sizes, heads,
    v_ref, k_ref, q_ref, ld_ref, g_ref,
    val_ref, kg_ref, qg_ref,
    within, wst, tv, lg, tw, states, adjoints, decays, ent, aft,
    own_f, own_b, total, f_in, f_out, b_in, b_out, acc, buf_a, buf_b,
    f_send, f_recv, b_send, b_recv, a_send, a_recv, x_send, x_recv,
):
    n_seq, n_head, n_sub = sizes
    length, cols = v_ref.shape
    state = k_ref.shape[1]
    channels = cols // heads
    count = length // BLOCK
    chunks = cols // LANES
    per = LANES // channels
    pad = wst.shape[1] // 2
    rows_out = length // (n_head * n_sub)
    blocks_out = rows_out // BLOCK
    s = lax.axis_index("seq")
    x = lax.axis_index("head")
    u = lax.axis_index("hsub")

    barrier = pltpu.get_barrier_semaphore()

    @pl.when(s > 0)
    def _():
        pl.semaphore_signal(barrier, inc=1, device_id={"seq": s - 1}, device_id_type=MESH)

    @pl.when(s < n_seq - 1)
    def _():
        pl.semaphore_signal(barrier, inc=1, device_id={"seq": s + 1}, device_id_type=MESH)

    for e in range(1, n_sub):
        pl.semaphore_signal(
            barrier, inc=1, device_id={"hsub": lax.rem(u + e, n_sub)}, device_id_type=MESH
        )
    for d in range(1, n_head):
        pl.semaphore_signal(
            barrier, inc=1, device_id={"head": lax.rem(x + d, n_head)}, device_id_type=MESH
        )

    def rows_of(c):
        return pl.ds(pl.multiple_of(c * BLOCK, BLOCK), BLOCK)

    row_at = lax.broadcasted_iota(jnp.int32, (BLOCK, BLOCK), 0)
    col_at = lax.broadcasted_iota(jnp.int32, (BLOCK, BLOCK), 1)
    upper = row_at <= col_at
    tri = jnp.where(upper, 1.0, 0.0).astype(WIDE)
    e_row = lax.broadcasted_iota(jnp.int32, (2 * pad, cols), 0)
    e_col = lax.broadcasted_iota(jnp.int32, (2 * pad, cols), 1)
    spread = jnp.where(lax.rem(e_row, pad) == e_col // channels, 1.0, 0.0).astype(LOW)
    lane_head = lax.broadcasted_iota(jnp.int32, (BLOCK, LANES), 1) // channels

    wst[...] = jnp.zeros_like(wst)
    own_f[...] = jnp.zeros_like(own_f)
    own_b[...] = jnp.zeros_like(own_b)
    total[...] = jnp.ones_like(total)

    def expand(slot, w):
        high = w.astype(LOW).astype(WIDE)
        wst[slot, 0:heads, :] = high
        wst[slot, pad:pad + heads, :] = w - high
        return product(wst[slot].astype(LOW), spread, (0, 0))

    def block_sums(c, _):
        rows = rows_of(c)
        w = lax.dot_general(
            ld_ref[:, rows], tri, (((1,), (0,)), ((), ())),
            precision=lax.Precision.HIGHEST, preferred_element_type=WIDE,
        )
        within[c] = w
        tail = expand(0, jnp.exp(w - w[:, BLOCK - 1:BLOCK]))
        lead = expand(1, jnp.exp(-w))
        tw[rows, :] = tail
        scaled_v = (tail * v_ref[rows, :].astype(WIDE)).astype(LOW)
        scaled_g = (lead * g_ref[rows, :].astype(WIDE)).astype(LOW)
        tv[rows, :] = scaled_v
        lg[rows, :] = scaled_g
        b = product(k_ref[rows, :], scaled_v, (0, 0))
        a = product(q_ref[rows, :], scaled_g, (0, 0))
        states[c] = b
        adjoints[c] = a
        for k in range(chunks):
            part = slice(k * LANES, (k + 1) * LANES)
            decay = lead[BLOCK - 1:BLOCK, part]
            decays[c, k] = decay
            own_f[k] = decay * own_f[k] + b[:, part]
            own_b[k] = own_b[k] + total[k] * a[:, part]
            total[k] = total[k] * decay
        return 0

    lax.fori_loop(0, count, block_sums, 0)

    def f_copy(k):
        return pltpu.make_async_remote_copy(
            src_ref=f_out.at[k], dst_ref=f_in.at[k], send_sem=f_send.at[k], recv_sem=f_recv.at[k],
            device_id={"seq": lax.rem(s + 1, n_seq)}, device_id_type=MESH,
        )

    def b_copy(k):
        return pltpu.make_async_remote_copy(
            src_ref=b_out.at[k], dst_ref=b_in.at[k], send_sem=b_send.at[k], recv_sem=b_recv.at[k],
            device_id={"seq": lax.rem(s + n_seq - 1, n_seq)}, device_id_type=MESH,
        )

    near = jnp.where(s > 0, 1, 0) + jnp.where(s < n_seq - 1, 1, 0) + (n_sub - 1) + (n_head - 1)
    pl.semaphore_wait(barrier, near)

    @pl.when(s == 0)
    def _():
        f_in[...] = jnp.zeros_like(f_in)

    @pl.when(s == n_seq - 1)
    def _():
        b_in[...] = jnp.zeros_like(b_in)

    if n_seq > 1:
        @pl.when(s == 0)
        def _():
            for k in range(chunks):
                f_out[k] = own_f[k]
                f_copy(k).start()

        @pl.when(s == n_seq - 1)
        def _():
            for k in range(chunks):
                b_out[k] = own_b[k]
                b_copy(k).start()

    f_at = jnp.minimum(3 * s, count - chunks)
    b_at = jnp.minimum(3 * (n_seq - 1 - s), count - chunks)

    def mask(wt, wt_t, h):
        return jnp.exp(jnp.minimum(wt_t[:, h:h + 1] - wt[h:h + 1, :], 0.0))

    def pair_work(c, _):
        rows = rows_of(c)
        wt = within[c]
        wt_t = wt.T
        pair_sum = jnp.zeros((BLOCK, BLOCK), WIDE)
        for p in range(chunks):
            part = slice(p * LANES, (p + 1) * LANES)
            v2 = v_ref[rows, part]
            g2 = g_ref[rows, part]
            stack = jnp.concatenate(
                [jnp.where(lane_head == r, v2, jnp.zeros_like(v2)) for r in range(per)], axis=0
            )
            pairs = product(stack, g2, (1, 1))
            for r in range(per):
                pair_sum += mask(wt, wt_t, p * per + r) * pairs[r * BLOCK:(r + 1) * BLOCK, :]
        pair_low = jnp.where(upper, pair_sum, 0.0).astype(LOW)
        acc[1, rows, :] = product(pair_low, q_ref[rows, :], (1, 0))
        acc[0, rows, :] = product(pair_low, k_ref[rows, :], (0, 0))

        if n_seq > 1:
            kf = c - f_at

            @pl.when((s > 0) & (kf >= 0) & (kf < chunks))
            def _():
                f_copy(kf).wait_recv()

                @pl.when(s < n_seq - 1)
                def _():
                    f_out[kf] = total[kf] * f_in[kf] + own_f[kf]
                    f_copy(kf).start()

            kb = c - b_at

            @pl.when((s < n_seq - 1) & (kb >= 0) & (kb < chunks))
            def _():
                b_copy(kb).wait_recv()

                @pl.when(s > 0)
                def _():
                    b_out[kb] = total[kb] * b_in[kb] + own_b[kb]
                    b_copy(kb).start()
        return 0

    lax.fori_loop(0, count, pair_work, 0)

    for k in range(chunks):
        part = slice(k * LANES, (k + 1) * LANES)

        def step(c, carry, k=k, part=part):
            f, b = carry
            e = count - 1 - c
            ent[c, :, part] = f.astype(LOW)
            aft[e, :, part] = b.astype(LOW)
            return (decays[c, k] * f + states[c, :, part], decays[e, k] * b + adjoints[e, :, part])

        lax.fori_loop(0, count, step, (f_in[k], b_in[k]))

    def carried(which, base):
        def one(t, _):
            c = base * blocks_out + t
            rows = rows_of(c)
            if which == 0:
                acc[0, rows, :] += product(lg[rows, :], ent[c], (1, 1))
            else:
                acc[1, rows, :] += product(tv[rows, :], aft[c], (1, 1))
            return 0

        lax.fori_loop(0, blocks_out, one, 0)

    def piece(base):
        return pl.ds(pl.multiple_of(base * rows_out, rows_out), rows_out)

    def a_copy(d, e, which):
        far = lax.rem(u + e, n_sub)
        base = lax.rem(x + d, n_head) * n_sub + far
        return pltpu.make_async_remote_copy(
            src_ref=acc.at[which, piece(base)], dst_ref=buf_a.at[d, e - 1, which],
            send_sem=a_send.at[d, e - 1, which], recv_sem=a_recv.at[d, e - 1, which],
            device_id={"hsub": far}, device_id_type=MESH,
        )

    def x_copy(d, which):
        far = lax.rem(x + d, n_head)
        return pltpu.make_async_remote_copy(
            src_ref=acc.at[which, piece(far * n_sub + u)], dst_ref=buf_b.at[d - 1, which],
            send_sem=x_send.at[d - 1, which], recv_sem=x_recv.at[d - 1, which],
            device_id={"head": far}, device_id_type=MESH,
        )

    order = list(range(1, n_head)) + [0]
    for d in order:
        far = lax.rem(x + d, n_head)
        for which in range(2):
            for e in range(1, n_sub):
                carried(which, far * n_sub + lax.rem(u + e, n_sub))
                a_copy(d, e, which).start()
        for which in range(2):
            carried(which, far * n_sub + u)
        for which in range(2):
            own = piece(far * n_sub + u)
            for e in range(1, n_sub):
                a_copy(d, e, which).wait_recv()
                acc[which, own, :] += buf_a[d, e - 1, which]
            if d > 0:
                x_copy(d, which).start()

    def value_work(c, _):
        rows = rows_of(c)
        wt = within[c]
        wt_t = wt.T
        key = k_ref[rows, :]
        scores = jnp.where(upper, product(key, q_ref[rows, :], (1, 1)), 0.0)
        back = product(key, aft[c], (1, 0)) * tw[rows, :]
        for p in range(chunks):
            part = slice(p * LANES, (p + 1) * LANES)
            g2 = g_ref[rows, part]
            mixed = jnp.concatenate(
                [(mask(wt, wt_t, p * per + r) * scores).astype(LOW) for r in range(per)], axis=1
            )
            stack = jnp.concatenate(
                [jnp.where(lane_head == r, g2, jnp.zeros_like(g2)) for r in range(per)], axis=0
            )
            val_ref[rows, part] = (product(mixed, stack, (1, 0)) + back[:, part]).astype(LOW)
        return 0

    lax.fori_loop(0, count, value_work, 0)

    mine = piece(x * n_sub + u)
    for which, out in ((0, qg_ref), (1, kg_ref)):
        result = acc[which, mine, :]
        for d in range(1, n_head):
            x_copy(d, which).wait_recv()
            result = result + buf_b[d - 1, which]
        out[...] = result

    for which in range(2):
        for d in range(n_head):
            for e in range(1, n_sub):
                a_copy(d, e, which).wait_send()
        for d in range(1, n_head):
            x_copy(d, which).wait_send()

    @pl.when(s < n_seq - 1)
    def _():
        for k in range(chunks):
            f_copy(k).wait_send()

    @pl.when(s > 0)
    def _():
        for k in range(chunks):
            b_copy(k).wait_send()


def local(sizes, token_values, key_proj, query_proj, log_decay, out_grad):
    n_seq, n_head, n_sub = sizes
    length, cols = token_values.shape
    heads = log_decay.shape[0]
    state = key_proj.shape[1]
    count = length // BLOCK
    chunks = cols // LANES
    pad = (heads + 7) // 8 * 8
    rows_out = length // (n_head * n_sub)
    vmem = pl.BlockSpec(memory_space=pltpu.VMEM)
    dma = pltpu.SemaphoreType.DMA
    subs = max(n_sub - 1, 1)
    fars = max(n_head - 1, 1)
    square = pltpu.VMEM((chunks, state, LANES), WIDE)
    value_grad, key_grad, query_grad = pl.pallas_call(
        functools.partial(kernel, sizes, heads),
        out_shape=(
            jax.ShapeDtypeStruct((length, cols), LOW),
            jax.ShapeDtypeStruct((rows_out, state), WIDE),
            jax.ShapeDtypeStruct((rows_out, state), WIDE),
        ),
        in_specs=[vmem] * 5,
        out_specs=(vmem, vmem, vmem),
        scratch_shapes=[
            pltpu.VMEM((count, heads, BLOCK), WIDE),
            pltpu.VMEM((2, 2 * pad, BLOCK), WIDE),
            pltpu.VMEM((length, cols), LOW),
            pltpu.VMEM((length, cols), LOW),
            pltpu.VMEM((length, cols), WIDE),
            pltpu.VMEM((count, state, cols), WIDE),
            pltpu.VMEM((count, state, cols), WIDE),
            pltpu.VMEM((count, chunks, 1, LANES), WIDE),
            pltpu.VMEM((count, state, cols), LOW),
            pltpu.VMEM((count, state, cols), LOW),
            square, square, pltpu.VMEM((chunks, 1, LANES), WIDE),
            square, square, square, square,
            pltpu.VMEM((2, length, state), WIDE),
            pltpu.VMEM((n_head, subs, 2, rows_out, state), WIDE),
            pltpu.VMEM((fars, 2, rows_out, state), WIDE),
            dma((chunks,)), dma((chunks,)), dma((chunks,)), dma((chunks,)),
            dma((n_head, subs, 2)), dma((n_head, subs, 2)),
            dma((fars, 2)), dma((fars, 2)),
        ],
        compiler_params=pltpu.CompilerParams(
            collective_id=0, has_side_effects=True, vmem_limit_bytes=56 * 1024 * 1024
        ),
    )(token_values, key_proj, query_proj, log_decay, out_grad)
    return value_grad, key_grad, query_grad


def solution(mesh):
    sizes = (mesh.shape["seq"], mesh.shape["head"], mesh.shape["hsub"])
    placed = (
        P(("groups", "seq"), ("head", "hsub")),
        P(("groups", "seq"), None),
        P(("groups", "seq"), None),
        P(("head", "hsub"), ("groups", "seq")),
        P(("groups", "seq"), ("head", "hsub")),
    )
    return jax.shard_map(
        functools.partial(local, sizes),
        mesh=mesh,
        in_specs=placed,
        out_specs=(
            P(("groups", "seq"), ("head", "hsub")),
            P(("groups", "seq", "head", "hsub"), None),
            P(("groups", "seq", "head", "hsub"), None),
        ),
        check_vma=False,
    )
```

time: 209 us -> 57.4 us (0.27); the launches traced: 207 us -> 57.3 us
  other arithmetic: 69.8 us -> 0 us
  Pallas kernels: 0 us -> 52.1 us
  matrix products: 46.1 us -> 0 us
  local copies, waits for them, and re-layouts: 45.1 us -> 4.51 us
  waiting for transfers between devices: 15.6 us -> 0 us
  between operations: 14.8 us -> 0.66 us
  blocking collectives: 13.7 us -> 0 us
    pallas_call x0 -> x1, Pallas kernels: none -> 52.1 us  [local(): pl.pallas_call(functools.partial(kernel, sizes, heads), out_shape=(jax.Sh...]
    dot_general x10 -> x0, matrix products: 46.1 us -> none  [the longest x1 8 us: local(): jnp.einsum('hcjn,cjhp->chnp', tail_keys, values, preferred_element_type=w...]
    add x32 -> x0, other arithmetic: 37.1 us -> none  [advance(): return (pieces[0][:, None, None] * carry + pieces[1], carry)]
    dynamic_update_slice x32 -> x0, other arithmetic: 27.2 us -> none  [local(): lax.scan(advance, zero_state, (decays, block_states))]
    reduce_scatter x2 -> x0, waiting for transfers between devices: 15.5 us -> none  [the longest x1 15.5 us: local(): lax.psum_scatter(key_part.reshape(length, state_size), ('head', 'hsub'),...]
    unnamed x24 -> x7, local copies, waits for them, and re-layouts: 19.6 us -> 4.51 us
    unnamed x1 -> x0, blocking collectives: 13.7 us -> none
    dynamic_slice x16 -> x0, local copies, waits for them, and re-layouts: 9.44 us -> none  [hop(): new = combine(before, jax.tree.map(lambda part: part[at], everything))]
  transfers between devices with their start and end apart: 4 -> 0, of which waited for: 1 -> 0; matrix products, arithmetic and copies ran while one was open for 52% -> 0% of each run, Pallas kernels for 0% -> 0%
where the time goes in v1:
time: 57.4 us; the launch traced here: 57.3 us
  Pallas kernels  52.1 us (91%)
  local copies, waits for them, and re-layouts  4.51 us (8%)
  between operations  0.66 us (1%)
    pallas_call x1, Pallas kernels, local(): pl.pallas_call(functools.partial(kernel, sizes, heads), out_shape=(jax.Sh...  52.1 us
    unnamed x7, local copies, waits for them, and re-layouts  4.51 us

profile of v1, /device:TPU:0, one launch (start us, length us, event | category | flops | bytes accessed | tf_op | source)
XLA Modules:
  0.0 57.3 jit_solution(3536538551789272488)
XLA Ops:
  0.6 52.1 %shard_map.76 = (bf16[2048,512]{1,0:T(8,128)(2,1)}, f32[512,128]{1,0:T(8,128)}, f32[512,128]{1,0:T(8,128)}) custom-call(bf16[2048,512]{1,0:T(8,128)(2,1)} %v_ref.1, bf16[2048,128]{1,0:T(8,128)(2,1)} %k_ref.1, bf16[2048,128]{1,0:T(8,128)(2,1)} %q_ref.1, f32[8,2048]{1,0:T(8,128)} %ld_ref.1, bf16[2048,512]{1,0:T(8,128)(2,1)} %g_ref.1), custom_call_target="tpu_custom_call" | custom-call | tf_op jit(solution)/shard_map/pallas_call | solution.py:322
  52.7 0.0 copy-start.1
  52.7 0.0 copy-start
  52.8 3.1 %copy.11 = bf16[2048,512]{1,0:T(8,128)(2,1)} copy(bf16[2048,512]{1,0:T(8,128)(2,1)} %get-tuple-element.6) | data formatting | bytes 4194304
  55.9 0.0 copy-done.1
  55.9 0.7 %copy.12 = f32[512,128]{1,0:T(8,128)} copy(f32[512,128]{1,0:T(8,128)S(1)} %copy-done.1) | data formatting | bytes 524288
  56.6 0.0 copy-done
  56.6 0.7 %copy.13 = f32[512,128]{1,0:T(8,128)} copy(f32[512,128]{1,0:T(8,128)S(1)} %copy-done) | data formatting | bytes 524288
Async XLA Ops:
  52.7 3.1 %copy-start.1 = (f32[512,128]{1,0:T(8,128)S(1)}, f32[512,128]{1,0:T(8,128)}, u32[]{:S(2)}) copy-start(f32[512,128]{1,0:T(8,128)} %get-tuple-element.7) | copy-start | bytes 786436
  52.7 3.8 %copy-start = (f32[512,128]{1,0:T(8,128)S(1)}, f32[512,128]{1,0:T(8,128)}, u32[]{:S(2)}) copy-start(f32[512,128]{1,0:T(8,128)} %get-tuple-element.8) | copy-start | bytes 786436

commit v2 on v1

--- a/solution.py
+++ b/solution.py
@@ -11,6 +11,8 @@
 WIDE = jnp.float32
 LOW = jnp.bfloat16
 MESH = pl.DeviceIdType.MESH
+UNROLL = 2
+DEEP = 4
 
 
 def product(a, b, over):
@@ -21,7 +23,7 @@
     sizes, heads,
     v_ref, k_ref, q_ref, ld_ref, g_ref,
     val_ref, kg_ref, qg_ref,
-    within, wst, tv, lg, tw, states, adjoints, decays, ent, aft,
+    within, wst, stacked, tv, lg, tw, states, adjoints, decays, ent, aft,
     own_f, own_b, total, f_in, f_out, b_in, b_out, acc, buf_a, buf_b,
     f_send, f_recv, b_send, b_recv, a_send, a_recv, x_send, x_recv,
 ):
@@ -32,7 +34,7 @@
     count = length // BLOCK
     chunks = cols // LANES
     per = LANES // channels
-    pad = wst.shape[1] // 2
+    pad = wst.shape[2] // 2
     rows_out = length // (n_head * n_sub)
     blocks_out = rows_out // BLOCK
     s = lax.axis_index("seq")
@@ -70,45 +72,56 @@
     spread = jnp.where(lax.rem(e_row, pad) == e_col // channels, 1.0, 0.0).astype(LOW)
     lane_head = lax.broadcasted_iota(jnp.int32, (BLOCK, LANES), 1) // channels
 
-    wst[...] = jnp.zeros_like(wst)
+    if heads < pad:
+        wst[...] = jnp.zeros_like(wst)
     own_f[...] = jnp.zeros_like(own_f)
     own_b[...] = jnp.zeros_like(own_b)
     total[...] = jnp.ones_like(total)
-
-    def expand(slot, w):
+    for c in range(count):
+        stacked[c * heads:(c + 1) * heads, :] = ld_ref[:, c * BLOCK:(c + 1) * BLOCK]
+    sums = lax.dot_general(
+        stacked[...], tri, (((1,), (0,)), ((), ())),
+        precision=lax.Precision.HIGHEST, preferred_element_type=WIDE,
+    )
+    for slot, w in enumerate((jnp.exp(sums - sums[:, BLOCK - 1:BLOCK]), jnp.exp(-sums))):
         high = w.astype(LOW).astype(WIDE)
-        wst[slot, 0:heads, :] = high
-        wst[slot, pad:pad + heads, :] = w - high
-        return product(wst[slot].astype(LOW), spread, (0, 0))
-
-    def block_sums(c, _):
-        rows = rows_of(c)
-        w = lax.dot_general(
-            ld_ref[:, rows], tri, (((1,), (0,)), ((), ())),
-            precision=lax.Precision.HIGHEST, preferred_element_type=WIDE,
-        )
-        within[c] = w
-        tail = expand(0, jnp.exp(w - w[:, BLOCK - 1:BLOCK]))
-        lead = expand(1, jnp.exp(-w))
-        tw[rows, :] = tail
-        scaled_v = (tail * v_ref[rows, :].astype(WIDE)).astype(LOW)
-        scaled_g = (lead * g_ref[rows, :].astype(WIDE)).astype(LOW)
-        tv[rows, :] = scaled_v
-        lg[rows, :] = scaled_g
-        b = product(k_ref[rows, :], scaled_v, (0, 0))
-        a = product(q_ref[rows, :], scaled_g, (0, 0))
-        states[c] = b
-        adjoints[c] = a
+        rest = w - high
+        for c in range(count):
+            wst[c, slot, 0:heads, :] = high[c * heads:(c + 1) * heads, :]
+            wst[c, slot, pad:pad + heads, :] = rest[c * heads:(c + 1) * heads, :]
+    for c in range(count):
+        within[c] = sums[c * heads:(c + 1) * heads, :]
+
+    def block_sums(t, _):
+        blocks = [t * DEEP + r for r in range(DEEP)]
+        rows = [rows_of(c) for c in blocks]
+        tails = [product(wst[c, 0].astype(LOW), spread, (0, 0)) for c in blocks]
+        leads = [product(wst[c, 1].astype(LOW), spread, (0, 0)) for c in blocks]
+        vs = [(w * v_ref[r, :].astype(WIDE)).astype(LOW) for w, r in zip(tails, rows)]
+        gs = [(w * g_ref[r, :].astype(WIDE)).astype(LOW) for w, r in zip(leads, rows)]
+        bs = [product(k_ref[r, :], scaled, (0, 0)) for scaled, r in zip(vs, rows)]
+        a_s = [product(q_ref[r, :], scaled, (0, 0)) for scaled, r in zip(gs, rows)]
         for k in range(chunks):
             part = slice(k * LANES, (k + 1) * LANES)
-            decay = lead[BLOCK - 1:BLOCK, part]
-            decays[c, k] = decay
-            own_f[k] = decay * own_f[k] + b[:, part]
-            own_b[k] = own_b[k] + total[k] * a[:, part]
-            total[k] = total[k] * decay
+            f, b, whole = own_f[k], own_b[k], total[k]
+            for r in range(DEEP):
+                decay = leads[r][BLOCK - 1:BLOCK, part]
+                decays[blocks[r], k] = decay
+                f = decay * f + bs[r][:, part]
+                b = b + whole * a_s[r][:, part]
+                whole = whole * decay
+            own_f[k] = f
+            own_b[k] = b
+            total[k] = whole
+        for r in range(DEEP):
+            tw[rows[r], :] = tails[r]
+            tv[rows[r], :] = vs[r]
+            lg[rows[r], :] = gs[r]
+            states[blocks[r]] = bs[r]
+            adjoints[blocks[r]] = a_s[r]
         return 0
 
-    lax.fori_loop(0, count, block_sums, 0)
+    lax.fori_loop(0, count // DEEP, block_sums, 0)
 
     def f_copy(k):
         return pltpu.make_async_remote_copy(
@@ -146,13 +159,14 @@
                 b_out[k] = own_b[k]
                 b_copy(k).start()
 
-    f_at = jnp.minimum(3 * s, count - chunks)
-    b_at = jnp.minimum(3 * (n_seq - 1 - s), count - chunks)
+    turns = count // UNROLL
+    f_at = jnp.minimum(3 * s - 2, turns - chunks)
+    b_at = jnp.minimum(3 * (n_seq - 1 - s) - 2, turns - chunks)
 
     def mask(wt, wt_t, h):
         return jnp.exp(jnp.minimum(wt_t[:, h:h + 1] - wt[h:h + 1, :], 0.0))
 
-    def pair_work(c, _):
+    def pair_rows(c):
         rows = rows_of(c)
         wt = within[c]
         wt_t = wt.T
@@ -168,34 +182,44 @@
             for r in range(per):
                 pair_sum += mask(wt, wt_t, p * per + r) * pairs[r * BLOCK:(r + 1) * BLOCK, :]
         pair_low = jnp.where(upper, pair_sum, 0.0).astype(LOW)
-        acc[1, rows, :] = product(pair_low, q_ref[rows, :], (1, 0))
-        acc[0, rows, :] = product(pair_low, k_ref[rows, :], (0, 0))
+        return product(pair_low, k_ref[rows, :], (0, 0)), product(pair_low, q_ref[rows, :], (1, 0))
+
+    def pair_work(c, _):
+        found = [pair_rows(c * UNROLL + r) for r in range(UNROLL)]
+        for r in range(UNROLL):
+            for which in range(2):
+                acc[which, rows_of(c * UNROLL + r), :] = found[r][which]
 
         if n_seq > 1:
             kf = c - f_at
 
-            @pl.when((s > 0) & (kf >= 0) & (kf < chunks))
+            @pl.when((s > 0) & (s < n_seq - 1) & (kf >= 0) & (kf < chunks))
             def _():
                 f_copy(kf).wait_recv()
-
-                @pl.when(s < n_seq - 1)
-                def _():
-                    f_out[kf] = total[kf] * f_in[kf] + own_f[kf]
-                    f_copy(kf).start()
+                f_out[kf] = total[kf] * f_in[kf] + own_f[kf]
+                f_copy(kf).start()
 
             kb = c - b_at
 
-            @pl.when((s < n_seq - 1) & (kb >= 0) & (kb < chunks))
+            @pl.when((s > 0) & (s < n_seq - 1) & (kb >= 0) & (kb < chunks))
             def _():
                 b_copy(kb).wait_recv()
-
-                @pl.when(s > 0)
-                def _():
-                    b_out[kb] = total[kb] * b_in[kb] + own_b[kb]
-                    b_copy(kb).start()
+                b_out[kb] = total[kb] * b_in[kb] + own_b[kb]
+                b_copy(kb).start()
         return 0
 
-    lax.fori_loop(0, count, pair_work, 0)
+    lax.fori_loop(0, count // UNROLL, pair_work, 0)
+
+    if n_seq > 1:
+        @pl.when(s == n_seq - 1)
+        def _():
+            for k in range(chunks):
+                f_copy(k).wait_recv()
+
+        @pl.when(s == 0)
+        def _():
+            for k in range(chunks):
+                b_copy(k).wait_recv()
 
     for k in range(chunks):
         part = slice(k * LANES, (k + 1) * LANES)
@@ -210,16 +234,14 @@
         lax.fori_loop(0, count, step, (f_in[k], b_in[k]))
 
     def carried(which, base):
-        def one(t, _):
-            c = base * blocks_out + t
-            rows = rows_of(c)
-            if which == 0:
-                acc[0, rows, :] += product(lg[rows, :], ent[c], (1, 1))
-            else:
-                acc[1, rows, :] += product(tv[rows, :], aft[c], (1, 1))
-            return 0
-
-        lax.fori_loop(0, blocks_out, one, 0)
+        left, right = ((lg, ent), (tv, aft))[which]
+        rows = [rows_of(base * blocks_out + r) for r in range(blocks_out)]
+        found = [
+            acc[which, rows[r], :] + product(left[rows[r], :], right[base * blocks_out + r], (1, 1))
+            for r in range(blocks_out)
+        ]
+        for r in range(blocks_out):
+            acc[which, rows[r], :] = found[r]
 
     def piece(base):
         return pl.ds(pl.multiple_of(base * rows_out, rows_out), rows_out)
@@ -258,13 +280,14 @@
             if d > 0:
                 x_copy(d, which).start()
 
-    def value_work(c, _):
+    def value_rows(c):
         rows = rows_of(c)
         wt = within[c]
         wt_t = wt.T
         key = k_ref[rows, :]
         scores = jnp.where(upper, product(key, q_ref[rows, :], (1, 1)), 0.0)
         back = product(key, aft[c], (1, 0)) * tw[rows, :]
+        found = []
         for p in range(chunks):
             part = slice(p * LANES, (p + 1) * LANES)
             g2 = g_ref[rows, part]
@@ -274,10 +297,17 @@
             stack = jnp.concatenate(
                 [jnp.where(lane_head == r, g2, jnp.zeros_like(g2)) for r in range(per)], axis=0
             )
-            val_ref[rows, part] = (product(mixed, stack, (1, 0)) + back[:, part]).astype(LOW)
+            found.append((product(mixed, stack, (1, 0)) + back[:, part]).astype(LOW))
+        return found
+
+    def value_work(c, _):
+        found = [value_rows(c * DEEP + r) for r in range(DEEP)]
+        for r in range(DEEP):
+            for p in range(chunks):
+                val_ref[rows_of(c * DEEP + r), p * LANES:(p + 1) * LANES] = found[r][p]
         return 0
 
-    lax.fori_loop(0, count, value_work, 0)
+    lax.fori_loop(0, count // DEEP, value_work, 0)
 
     mine = piece(x * n_sub + u)
     for which, out in ((0, qg_ref), (1, kg_ref)):
@@ -322,15 +352,16 @@
     value_grad, key_grad, query_grad = pl.pallas_call(
         functools.partial(kernel, sizes, heads),
         out_shape=(
-            jax.ShapeDtypeStruct((length, cols), LOW),
-            jax.ShapeDtypeStruct((rows_out, state), WIDE),
-            jax.ShapeDtypeStruct((rows_out, state), WIDE),
+            pltpu.VMEM((length, cols), LOW),
+            pltpu.VMEM((rows_out, state), WIDE),
+            pltpu.VMEM((rows_out, state), WIDE),
         ),
         in_specs=[vmem] * 5,
         out_specs=(vmem, vmem, vmem),
         scratch_shapes=[
             pltpu.VMEM((count, heads, BLOCK), WIDE),
-            pltpu.VMEM((2, 2 * pad, BLOCK), WIDE),
+            pltpu.VMEM((count, 2, 2 * pad, BLOCK), WIDE),
+            pltpu.VMEM((count * heads, BLOCK), WIDE),
             pltpu.VMEM((length, cols), LOW),
             pltpu.VMEM((length, cols), LOW),
             pltpu.VMEM((length, cols), WIDE),

time: 57.4 us -> 43.8 us (0.76)
  Pallas kernels: 52.1 us -> 40.3 us
  local copies, waits for them, and re-layouts: 4.51 us -> 2.73 us
    pallas_call x1, Pallas kernels: 52.1 us -> 40.3 us  [local(): pl.pallas_call(functools.partial(kernel, sizes, heads), out_shape=(pltpu....]
    unnamed x7 -> x3, local copies, waits for them, and re-layouts: 4.51 us -> 2.73 us
where the time goes in v2:
time: 43.8 us; the launch traced here: 43.6 us
  Pallas kernels  40.3 us (92%)
  local copies, waits for them, and re-layouts  2.73 us (6%)
  between operations  0.64 us (1%)
    pallas_call x1, Pallas kernels, local(): pl.pallas_call(functools.partial(kernel, sizes, heads), out_shape=(pltpu....  40.3 us
    unnamed x3, local copies, waits for them, and re-layouts  2.73 us

profile of v2, /device:TPU:0, one launch (start us, length us, event | category | flops | bytes accessed | tf_op | source)
XLA Modules:
  0.0 43.6 jit_solution(15320388919432057768)
XLA Ops:
  0.6 40.3 %shard_map.76 = (bf16[2048,512]{1,0:T(8,128)(2,1)S(1)}, f32[512,128]{1,0:T(8,128)S(1)}, f32[512,128]{1,0:T(8,128)S(1)}) custom-call(bf16[2048,512]{1,0:T(8,128)(2,1)} %v_ref.1, bf16[2048,128]{1,0:T(8,128)(2,1)} %k_ref.1, bf16[2048,128]{1,0:T(8,128)(2,1)} %q_ref.1, f32[8,2048]{1,0:T(8,128)} %ld_ref.1, bf16[2048,512]{1,0:T(8,128)(2,1)} %g_ref.1), custom_call_target="tpu_custom_call" | custom-call | tf_op jit(solution)/shard_map/pallas_call | solution.py:352
  40.9 1.3 %copy.11 = bf16[2048,512]{1,0:T(8,128)(2,1)} copy(bf16[2048,512]{1,0:T(8,128)(2,1)S(1)} %get-tuple-element.3) | data formatting | bytes 4194304
  42.2 0.7 %copy.12 = f32[512,128]{1,0:T(8,128)} copy(f32[512,128]{1,0:T(8,128)S(1)} %get-tuple-element.4) | data formatting | bytes 524288
  42.9 0.7 %copy.13 = f32[512,128]{1,0:T(8,128)} copy(f32[512,128]{1,0:T(8,128)S(1)} %get-tuple-element.5) | data formatting | bytes 524288

commit v3 on v2

--- a/solution.py
+++ b/solution.py
@@ -272,7 +272,6 @@
                 a_copy(d, e, which).start()
         for which in range(2):
             carried(which, far * n_sub + u)
-        for which in range(2):
             own = piece(far * n_sub + u)
             for e in range(1, n_sub):
                 a_copy(d, e, which).wait_recv()

time: 43.8 us -> 43.5 us (level)
  no operation moved by 1% of the time
where the time goes in v3:
time: 43.5 us; the launch traced here: 43.4 us
  Pallas kernels  40 us (92%)
  local copies, waits for them, and re-layouts  2.73 us (6%)
  between operations  0.64 us (1%)
    pallas_call x1, Pallas kernels, local(): pl.pallas_call(functools.partial(kernel, sizes, heads), out_shape=(pltpu....  40 us
    unnamed x3, local copies, waits for them, and re-layouts  2.73 us

profile of v3, /device:TPU:0, one launch (start us, length us, event | category | flops | bytes accessed | tf_op | source)
XLA Modules:
  0.0 43.4 jit_solution(3375231642411313314)
XLA Ops:
  0.6 40.0 %shard_map.76 = (bf16[2048,512]{1,0:T(8,128)(2,1)S(1)}, f32[512,128]{1,0:T(8,128)S(1)}, f32[512,128]{1,0:T(8,128)S(1)}) custom-call(bf16[2048,512]{1,0:T(8,128)(2,1)} %v_ref.1, bf16[2048,128]{1,0:T(8,128)(2,1)} %k_ref.1, bf16[2048,128]{1,0:T(8,128)(2,1)} %q_ref.1, f32[8,2048]{1,0:T(8,128)} %ld_ref.1, bf16[2048,512]{1,0:T(8,128)(2,1)} %g_ref.1), custom_call_target="tpu_custom_call" | custom-call | tf_op jit(solution)/shard_map/pallas_call | solution.py:351
  40.6 1.3 %copy.11 = bf16[2048,512]{1,0:T(8,128)(2,1)} copy(bf16[2048,512]{1,0:T(8,128)(2,1)S(1)} %get-tuple-element.3) | data formatting | bytes 4194304
  41.9 0.7 %copy.12 = f32[512,128]{1,0:T(8,128)} copy(f32[512,128]{1,0:T(8,128)S(1)} %get-tuple-element.4) | data formatting | bytes 524288
  42.7 0.7 %copy.13 = f32[512,128]{1,0:T(8,128)} copy(f32[512,128]{1,0:T(8,128)S(1)} %get-tuple-element.5) | data formatting | bytes 524288
